TPU v7x, 128 devices: a whole 4x4x4 slice. The times are simulated.
128 devices in a mesh: ctx: 8 (over y, x_hi), head: 16 (over x_lo, z, core).
Axes of the slice: x: 4 (x_hi: 2, x_lo: 2; x = x_hi * 2 + x_lo), y: 4, z: 4, core: 2. Of those that a mesh axis runs over, the one named last changes fastest.
Arguments:
- query: bfloat16 [16384, 32, 128], P(('ctx', 'head')), may hold values from -6 to 6
- keys: bfloat16 [16384, 32, 128], P(('ctx', 'head')), may hold values from -6 to 6
- values: bfloat16 [16384, 32, 128], P(('ctx', 'head')), may hold values from -6 to 6
- grad_out: bfloat16 [16384, 32, 128], P(('ctx', 'head')), may hold values from -6 to 6
- window: int32 [32], P('head'), may hold values from 1 to 8, as said below
- global_blocks: int32 [6], replicated, may hold values from 0 to 127, as said below
Outputs:
- attended: bfloat16 [16384, 32, 128], P(('ctx', 'head'))
- grad_query: bfloat16 [16384, 32, 128], P(('ctx', 'head'))
- grad_keys: bfloat16 [16384, 32, 128], P(('ctx', 'head'))
- grad_values: bfloat16 [16384, 32, 128], P(('ctx', 'head'))
Inputs may be any that keep to these rules, and one draw needn't show every extreme that they name: Some head has a window of exactly 8 blocks. `global_blocks`: 6 distinct block indices; blocks 0 and 127 are always among them.
All inputs are finite; a program needn't handle non-finite values.
Results may differ from a plain program's by a relative error of at most 0.019.
Values may be sent and summed in bfloat16 or wider, within the bound.
No kernel may reach another device: no remote copies, remote signals or barrier semaphores. Data moves between devices by JAX's collectives and lax.ppermute only.
A program may use at most 128 MiB of HBM per device.

v0:
```python
import functools

import jax
import jax.numpy as jnp
from jax import lax
from jax.experimental import pallas as pl
from jax.experimental.pallas import tpu as pltpu
from jax.sharding import Mesh, PartitionSpec as P

BLK = 128
HD = 128
WIN = 8
HALO = WIN - 1
RUN = 16
EXT = HALO + RUN
GLOB = 6
BAND = WIN + 1
UNIT = 3
PART = 3
NEG = -1e30
SCALE = HD ** -0.5
LOG2E = 1.4426950408889634
GROUP = ("xh", "xl", "z", "c")
F32 = jnp.float32
BF16 = jnp.bfloat16


def dot(a, b):
    return jnp.dot(a, b, preferred_element_type=F32)


def attention_kernel(
    info, kv, qd, halo_a, halo_b, glob,
    odq, own, back_a, back_b, glob_grad,
    kx, vx, kt, vt, kgt, vgt, qs, dos, st, pb, ds, pg, dg, dkg, dvg, tail, head,
):
    w = info[0]
    last_y = info[1]
    for h in range(HALO):
        kx[0, h] = halo_a[h, 0]
        vx[0, h] = halo_a[h, 1]
        kx[1, h] = halo_b[h, 0]
        vx[1, h] = halo_b[h, 1]

    @pl.when(last_y == 1)
    def _():
        for h in range(HALO):
            kx[1, h] = kv[17 + h, 0]
            vx[1, h] = kv[17 + h, 1]

    for t in range(RUN):
        for ch in range(2):
            p = place(ch, t)
            kx[ch, HALO + t] = kv[p, 0]
            vx[ch, HALO + t] = kv[p, 1]
    for e in range(EXT):
        for ch in range(2):
            kt[ch, :, e * BLK:(e + 1) * BLK] = kx[ch, e].T
            vt[ch, :, e * BLK:(e + 1) * BLK] = vx[ch, e].T
    for s in range(GLOB):
        kgt[:, s * BLK:(s + 1) * BLK] = glob[s, 0].T
        vgt[:, s * BLK:(s + 1) * BLK] = glob[s, 1].T

    upper = lax.broadcasted_iota(jnp.int32, (1, 2 * BLK), 1) // BLK
    lane_full = lax.broadcasted_iota(jnp.int32, (BLK, 2 * BLK), 1)
    row_full = lax.broadcasted_iota(jnp.int32, (BLK, 2 * BLK), 0)
    c = SCALE * LOG2E
    cut = BAND * BLK

    def tile(ch, tt, slot, wide):
        t0 = 2 * tt
        seg = tt // 4
        pos = jnp.where(ch == 0, seg * 16, 24 - seg * 16) + t0 - seg * 8
        first = info[2 + ch] + t0
        q = qd[pl.ds(pos, 2), 0].reshape(2 * BLK, HD)
        do = qd[pl.ds(pos, 2), 1].reshape(2 * BLK, HD)
        qt = q.T
        dot_ = do.T

        def allowed(r):
            if r < BAND:
                return jnp.logical_and(HALO - r + upper < w, first - HALO + r >= 0)
            return info[4 + r - BAND] <= first + upper - w

        keep = {}

        def source(ref, which, r, n):
            if r < BAND:
                return ref[ch, pl.ds(t0 + r, n)].reshape(n * BLK, HD)
            return glob[r - BAND:r - BAND + n, which].reshape(n * BLK, HD)

        def probs(r, n):
            if r < BAND:
                return pb.at[tt, r * BLK:(r + n) * BLK]
            return pg.at[slot, (r - BAND) * BLK:(r - BAND + n) * BLK]

        def grads(r, n):
            if r < BAND:
                return ds.at[tt, r * BLK:(r + n) * BLK]
            return dg.at[slot, (r - BAND) * BLK:(r - BAND + n) * BLK]

        def scores(first_r, n):
            big = dot(source(kx, 0, first_r, n), qt)
            for k in range(n):
                r = first_r + k
                s = big[k * BLK:(k + 1) * BLK]
                if HALO <= r < BAND:
                    s = jnp.where(row_full <= lane_full - BLK * (r - HALO), s, NEG)
                st[slot, r * BLK:(r + 1) * BLK] = s
                here = jnp.max(s.reshape(BLK // 8, 8, 2 * BLK), axis=0)
                here = jnp.where(allowed(r), here, NEG)
                keep["top"] = jnp.maximum(keep["top"], here) if r else here

        def after_scores():
            keep["top"] = jnp.max(keep["top"], axis=0, keepdims=True) * c

        def weigh(first_r, n):
            for k in range(n):
                r = first_r + k
                off = jnp.where(allowed(r), keep["top"], -NEG)
                e = jnp.exp2(st[slot, r * BLK:(r + 1) * BLK] * c - off)
                here = jnp.sum(e.reshape(BLK // 8, 8, 2 * BLK), axis=0)
                keep["total"] = keep["total"] + here if r else here
                probs(first_r, n)[k * BLK:(k + 1) * BLK] = e.astype(BF16)

        cols = pl.ds(pl.multiple_of(t0 * BLK, 2 * BLK), cut)

        def attend():
            keep["inv"] = inv = 1.0 / jnp.sum(keep["total"], axis=0, keepdims=True)
            ot = dot(vt[ch, :, cols], pb[tt])
            if wide:
                ot = ot + dot(vgt[:, :wide], pg[slot, :wide])
            ot = ot * inv
            ob = ot.astype(BF16)
            dof = dot_.astype(F32)
            keep["delta"] = jnp.sum(ob.astype(F32) * dof, axis=0, keepdims=True)
            odq[pl.ds(pos, 2), 0] = ob.T.reshape(2, BLK, HD)
            col = jnp.broadcast_to(inv, (8, 2 * BLK)).T[:, :1]
            qs[tt] = (q.astype(F32) * col).astype(BF16)
            dos[tt] = (do.astype(F32) * col).astype(BF16)

        def back(r, n):
            g = dot(source(vx, 1, r, n), dot_) - keep["delta"]
            grads(r, n)[...] = (probs(r, n)[...].astype(F32) * g).astype(BF16)

        def finish_tile():
            dqt = dot(kt[ch, :, cols], ds[tt])
            if wide:
                dqt = dqt + dot(kgt[:, :wide], dg[slot, :wide])
            dqt = dqt * (keep["inv"] * SCALE)
            odq[pl.ds(pos, 2), 1] = dqt.astype(BF16).T.reshape(2, BLK, HD)

        return scores, after_scores, weigh, attend, back, finish_tile

    dkg[...] = jnp.zeros_like(dkg)
    dvg[...] = jnp.zeros_like(dvg)

    def group(ch, i, parts):
        wide = parts * PART * BLK
        segs = [(r, UNIT) for r in range(0, BAND, UNIT)] + [(BAND + PART * k, PART) for k in range(parts)]
        stages = [tile(ch, 4 * i + k, k, wide) for k in range(4)]
        scores, after_scores, weigh, attend, back, finish_tile = zip(*stages)
        for seg in segs:
            for f in scores:
                f(*seg)
        for f in after_scores:
            f()
        for seg in segs:
            for f in weigh:
                f(*seg)
        for f in attend:
            f()
        for seg in segs:
            for f in back:
                f(*seg)
        for f in finish_tile:
            f()
        if parts:
            for weights, rows_of, total in ((dg, qs, dkg), (pg, dos, dvg)):
                acc = total[:wide]
                for k in range(4):
                    acc = acc + dot(weights[k, :wide], rows_of[4 * i + k])
                total[:wide] = acc

    def run(ch, outer):
        def step(i, carry):
            last = info[2 + ch] + 8 * i + 7
            count = (info[4] <= last - w).astype(jnp.int32)
            for g in range(1, GLOB):
                count += (info[4 + g] <= last - w).astype(jnp.int32)
            needed = (count + PART - 1) // PART
            for parts in range(GLOB // PART + 1):
                @pl.when(needed == parts)
                def _(parts=parts):
                    group(ch, i, parts)
            return carry

        lax.fori_loop(0, RUN // 8, step, 0)

        for u in range((EXT + 1) // 2):
            for part, (weights, rows_of) in enumerate(((ds, qs), (pb, dos))):
                acc = [None, None]
                for tt in range(max(0, u - 4), min(RUN // 2, u + 1)):
                    r = 2 * (u - tt)
                    n = min(2, BAND - r)
                    if n == 2:
                        g = dot(weights[tt, r * BLK:(r + 2) * BLK], rows_of[tt])
                        g = [g[:BLK], g[BLK:]]
                    else:
                        g = [dot(weights[tt, r * BLK:(r + 1) * BLK], rows_of[tt])]
                    for k in range(n):
                        acc[k] = g[k] if acc[k] is None else acc[k] + g[k]
                for k in range(2):
                    e = 2 * u + k
                    if e >= EXT or acc[k] is None:
                        continue
                    g = acc[k] * SCALE if part == 0 else acc[k]
                    if e < HALO:
                        head[ch, e, part] = g
                    else:
                        t = e - HALO
                        own[jnp.where(ch == 0, place(0, t), place(1, t)), part] = g.astype(BF16)
                    if e >= RUN:
                        tail[ch, e - RUN, part] = g
        return outer

    lax.fori_loop(0, 2, run, 0)
    for h in range(HALO):
        back_a[h] = head[0, h].astype(BF16)
        back_b[h] = head[1, h].astype(BF16)

    @pl.when(last_y == 1)
    def _():
        for h in range(HALO):
            own[17 + h] = (tail[0, h] + head[1, h]).astype(BF16)

    for s in range(GLOB):
        glob_grad[s, 0] = (dkg[s * BLK:(s + 1) * BLK] * SCALE).astype(BF16)
        glob_grad[s, 1] = dvg[s * BLK:(s + 1) * BLK].astype(BF16)


def place(ch, t):
    return (t // 8) * 16 + t % 8 if ch == 0 else (1 - t // 8) * 16 + 8 + t % 8


def vmem():
    return pl.BlockSpec(memory_space=pltpu.VMEM)


def attention(info, kv, qd, halo_a, halo_b, glob):
    sds = jax.ShapeDtypeStruct
    return pl.pallas_call(
        attention_kernel,
        out_shape=(
            sds((32, 2, BLK, HD), BF16),
            sds((32, 2, BLK, HD), BF16),
            sds((HALO, 2, BLK, HD), BF16),
            sds((HALO, 2, BLK, HD), BF16),
            sds((GLOB, 2, BLK, HD), BF16),
        ),
        in_specs=[pl.BlockSpec(memory_space=pltpu.SMEM)] + [vmem()] * 5,
        out_specs=(vmem(),) * 5,
        scratch_shapes=[
            pltpu.VMEM((2, EXT, BLK, HD), BF16),
            pltpu.VMEM((2, EXT, BLK, HD), BF16),
            pltpu.VMEM((2, HD, EXT * BLK + BLK), BF16),
            pltpu.VMEM((2, HD, EXT * BLK + BLK), BF16),
            pltpu.VMEM((HD, GLOB * BLK), BF16),
            pltpu.VMEM((HD, GLOB * BLK), BF16),
            pltpu.VMEM((RUN // 2, 2 * BLK, HD), BF16),
            pltpu.VMEM((RUN // 2, 2 * BLK, HD), BF16),
            pltpu.VMEM((4, (BAND + GLOB) * BLK, 2 * BLK), F32),
            pltpu.VMEM((RUN // 2, BAND * BLK, 2 * BLK), BF16),
            pltpu.VMEM((RUN // 2, BAND * BLK, 2 * BLK), BF16),
            pltpu.VMEM((4, GLOB * BLK, 2 * BLK), BF16),
            pltpu.VMEM((4, GLOB * BLK, 2 * BLK), BF16),
            pltpu.VMEM((GLOB * BLK, HD), F32),
            pltpu.VMEM((GLOB * BLK, HD), F32),
            pltpu.VMEM((2, HALO, 2, BLK, HD), F32),
            pltpu.VMEM((2, HALO, 2, BLK, HD), F32),
        ],
        compiler_params=pltpu.CompilerParams(vmem_limit_bytes=52 * 2**20),
        cost_estimate=pl.CostEstimate(
            flops=12 * 448 * BLK**3, bytes_accessed=16 * 2**20, transcendentals=448 * BLK * BLK
        ),
        name="attention",
    )(info, kv, qd, halo_a, halo_b, glob)


def finish_kernel(info, own, back_a, back_b, glob_one, glob_two, out):
    for p in range(32):
        if 17 <= p < 24:
            out[p] = (own[p].astype(F32) + back_a[p - 17].astype(F32)).astype(BF16)
        elif 9 <= p < 16:
            out[p] = (own[p].astype(F32) + back_b[p - 9].astype(F32)).astype(BF16)
        else:
            out[p] = own[p]
    for s in range(GLOB):
        @pl.when(info[16 + s] == 1)
        def _(s=s):
            p = info[10 + s]
            ia = jnp.clip(p - 17, 0, HALO - 1)
            ib = jnp.clip(p - 9, 0, HALO - 1)
            in_a = jnp.logical_and(p >= 17, p < 24)
            in_b = jnp.logical_and(p >= 9, p < 16)
            g = own[p].astype(F32) + glob_one[s].astype(F32) + glob_two[s].astype(F32)
            g = g + jnp.where(in_a, back_a[ia].astype(F32), 0.0)
            g = g + jnp.where(in_b, back_b[ib].astype(F32), 0.0)
            out[p] = g.astype(BF16)


def finish(info, own, back_a, back_b, glob_one, glob_two):
    return pl.pallas_call(
        finish_kernel,
        out_shape=jax.ShapeDtypeStruct((32, 2, BLK, HD), BF16),
        in_specs=[pl.BlockSpec(memory_space=pltpu.SMEM)] + [vmem()] * 5,
        out_specs=vmem(),
        compiler_params=pltpu.CompilerParams(vmem_limit_bytes=16 * 2**20),
        cost_estimate=pl.CostEstimate(flops=2**21, bytes_accessed=6 * 2**20, transcendentals=0),
        name="finish",
    )(info, own, back_a, back_b, glob_one, glob_two)


def to_heads(x, y):
    pair = jnp.stack([x, y], axis=0).reshape(2, BLK, 16, 2, HD)
    pair = jnp.transpose(pair, (3, 2, 0, 1, 4)).reshape(32, 2, BLK, HD)
    return pair


def to_rows(pair):
    pair = pair.reshape(2, 16, 2, BLK, HD)
    pair = jnp.transpose(pair, (2, 3, 1, 0, 4)).reshape(2, BLK, 32, HD)
    return pair[0], pair[1]


def exchange(x):
    return lax.all_to_all(x, GROUP, 0, 0, tiled=True)


PAIR_ONE = [(0, 1), (1, 0), (2, 3), (3, 2)]
PAIR_TWO = [(1, 2), (2, 1), (3, 0), (0, 3)]


def shards(query, keys, values, grad_out, window, global_blocks):
    me = lax.axis_index("y")
    w = jnp.where(lax.axis_index("xh") == 0, window[0], window[1])
    before = global_blocks[None, :] < global_blocks[:, None]
    rank = jnp.sum(before.astype(jnp.int32), axis=1)
    chosen = rank[None, :] == jnp.arange(GLOB, dtype=jnp.int32)[:, None]
    global_blocks = jnp.sum(jnp.where(chosen, global_blocks[None, :], 0), axis=1)
    low = global_blocks < 64
    owner = jnp.where(low, global_blocks // RUN, (127 - global_blocks) // RUN)
    t = global_blocks % RUN
    where = jnp.where(low, (t // 8) * 16 + t % 8, (1 - t // 8) * 16 + 8 + t % 8)
    info = jnp.concatenate([
        jnp.stack([w, (me == 3).astype(jnp.int32), RUN * me, 112 - RUN * me]),
        global_blocks, where, (owner == me).astype(jnp.int32),
    ]).astype(jnp.int32)

    kv = exchange(to_heads(keys, values))
    qd = exchange(to_heads(query, grad_out))

    halo_a = lax.ppermute(kv[17:24], "y", [(0, 1), (1, 2), (2, 3)])
    halo_b = lax.ppermute(kv[9:16], "y", [(3, 2), (2, 1), (1, 0)])
    mine = jnp.concatenate([lax.dynamic_slice_in_dim(kv, where[s], 1, 0) for s in range(GLOB)], axis=0)
    other = lax.ppermute(mine, "y", PAIR_ONE)
    mine = jnp.where((owner == me)[:, None, None, None], mine, other)
    other = lax.ppermute(mine, "y", PAIR_TWO)
    glob = jnp.where((owner // 2 == me // 2)[:, None, None, None], mine, other)

    odq, own, back_a, back_b, glob_grad = attention(info, kv, qd, halo_a, halo_b, glob)

    odq = exchange(odq)
    back_a = lax.ppermute(back_a, "y", [(1, 0), (2, 1), (3, 2)])
    back_b = lax.ppermute(back_b, "y", [(0, 1), (1, 2), (2, 3)])
    other = lax.ppermute(glob_grad, "y", PAIR_ONE)
    glob_grad = (glob_grad.astype(F32) + other.astype(F32)).astype(BF16)
    other = lax.ppermute(glob_grad, "y", PAIR_TWO)
    dkv = exchange(finish(info, own, back_a, back_b, glob_grad, other))
    attended, grad_query = to_rows(odq)
    grad_keys, grad_values = to_rows(dkv)
    return attended, grad_query, grad_keys, grad_values


def solution(mesh):
    fine = Mesh(mesh.devices.reshape(4, 2, 2, 4, 2), ("y", "xh", "xl", "z", "c"))
    rows = P(("y", "xh", "xl", "z", "c"), None, None)
    return jax.shard_map(
        shards,
        mesh=fine,
        in_specs=(rows, rows, rows, rows, P(("xl", "z", "c")), P()),
        out_specs=(rows,) * 4,
        check_vma=False,
    )
```

profile of v0, /device:TPU:1, one launch (start us, length us, event | category | flops | bytes accessed | tf_op | source)
XLA Modules:
  0.0 185.6 jit_solution(17097534217164264470)
XLA Ops:
  0.6 1.7 copy.18
  2.4 0.4 copy.19
  2.8 1.5 pad_maximum_fusion
  4.3 9.6 %all-to-all-start = ((bf16[32,2,128,128]{3,2,1,0:T(8,128)(2,1)}), bf16[32,2,128,128]{3,2,1,0:T(8,128)(2,1)S(1)}, u32[]{:S(2)}, u32[]{:S(2)}) async-start(bf16[32,2,128,128]{3,2,1,0:T(8,128)(2,1)} %bitcast.9), calls=%async_computation | async-start | bytes 4194304 | tf_op jit(solution)/shard_map/all_to_all | solution.py:337
  13.9 0.2 convert_reduce_fusion
  14.1 0.1 select_reduce_fusion
  14.2 0.6 fusion.5
  22.5 1.6 copy.20
  24.1 2.6 %copy.21 = bf16[1,128,16,2,128]{4,1,0,2,3:T(8,128)(2,1)} copy(bf16[1,128,16,2,128]{4,3,2,1,0:T(2,128)(2,1)} %bitcast.36) | data formatting | bytes 2097152 | tf_op jit(solution)/shard_map/stack | solution.py:325
  30.6 2.8 %pad_maximum_fusion.1 = bf16[2,128,16,2,128]{4,1,0,2,3:T(8,128)(2,1)} fusion(bf16[1,128,16,2,128]{4,1,0,2,3:T(8,128)(2,1)} %copy.21, bf16[1,128,16,2,128]{4,1,0,2,3:T(8,128)(2,1)S(1)} %copy.20), kind=kLoop, calls=%fused_computation.1 | loop fusion | flops 1048576 | bytes 4194304 | tf_op jit(solution)/shard_map/stack | solution.py:325
  33.4 8.8 %all-to-all-done.kv = bf16[32,2,128,128]{3,2,1,0:T(8,128)(2,1)S(1)} async-done(((bf16[32,2,128,128]{3,2,1,0:T(8,128)(2,1)}), bf16[32,2,128,128]{3,2,1,0:T(8,128)(2,1)S(1)}, u32[]{:S(2)}, u32[]{:S(2)}) %all-to-all-start) | async-done | bytes 2097184 | tf_op jit(solution)/shard_map/all_to_all | solution.py:337
  42.2 5.2 %all-to-all-start.1 = ((bf16[32,2,128,128]{3,2,1,0:T(8,128)(2,1)}), bf16[32,2,128,128]{3,2,1,0:T(8,128)(2,1)}, u32[]{:S(2)}, u32[]{:S(2)}) async-start(bf16[32,2,128,128]{3,2,1,0:T(8,128)(2,1)} %bitcast.13), calls=%async_computation.1 | async-start | bytes 4194304 | tf_op jit(solution)/shard_map/all_to_all | solution.py:337
  47.4 0.0 copy-start.3
  47.6 1.4 collective-permute-start.2
  49.0 9.0 %collective-permute-done.2 = bf16[6,2,128,128]{3,2,1,0:T(8,128)(2,1)S(1)} collective-permute-done((bf16[6,2,128,128]{3,2,1,0:T(8,128)(2,1)S(1)}, bf16[6,2,128,128]{3,2,1,0:T(8,128)(2,1)S(1)}, u32[]{:S(2)}, u32[]{:S(2)}) %collective-permute-start.2) | collective-permute-done | bytes 393248 | tf_op jit(solution)/shard_map/ppermute | solution.py:366
  58.0 0.1 broadcast_select_fusion
  58.1 2.8 %collective-permute-start.3 = (bf16[6,2,128,128]{3,2,1,0:T(8,128)(2,1)S(1)}, bf16[6,2,128,128]{3,2,1,0:T(8,128)(2,1)}, u32[]{:S(2)}, u32[]{:S(2)}) collective-permute-start(bf16[6,2,128,128]{3,2,1,0:T(8,128)(2,1)S(1)} %broadcast_select_fusion), channel_id=1, source_target_pairs={{32,64},{64,32},{96,0},{0,96},{33,65},{65,33},{97,1},{1,97},{34,66... | collective-permute-start | bytes 1179656 | tf_op jit(solution)/shard_map/ppermute | solution.py:368
  60.9 0.1 fusion.4
  61.0 1.3 collective-permute-start.1
  62.3 4.0 %collective-permute-start = (bf16[7,2,128,128]{3,2,1,0:T(8,128)(2,1)S(1)}, bf16[7,2,128,128]{3,2,1,0:T(8,128)(2,1)S(1)}, u32[]{:S(2)}, u32[]{:S(2)}) collective-permute-start(bf16[7,2,128,128]{3,2,1,0:T(8,128)(2,1)S(1)} %get-tuple-element.23), channel_id=1, source_target_pairs={{0,32},{32,64},{64,96},{1,33},{33,65},{65,97},{2,34},{34,66},{66,9... | collective-permute-start | bytes 1376264 | tf_op jit(solution)/shard_map/ppermute | solution.py:363
  66.4 0.6 fusion.6
  68.3 0.1 concatenate.8.info
  68.3 0.8 collective-permute-done.3
  69.1 1.1 broadcast_select_fusion.1.glob
  70.2 5.6 %all-to-all-done.1.qd = bf16[32,2,128,128]{3,2,1,0:T(8,128)(2,1)} async-done(((bf16[32,2,128,128]{3,2,1,0:T(8,128)(2,1)}), bf16[32,2,128,128]{3,2,1,0:T(8,128)(2,1)}, u32[]{:S(2)}, u32[]{:S(2)}) %all-to-all-start.1) | async-done | bytes 2097184 | tf_op jit(solution)/shard_map/all_to_all | solution.py:337
  75.8 0.0 collective-permute-done.1.halo_b
  75.8 0.8 copy-done.4
  76.6 0.8 copy-done.5
  77.4 31.6 %attention.1 = (bf16[32,2,128,128]{3,2,1,0:T(8,128)(2,1)}, bf16[32,2,128,128]{3,2,1,0:T(8,128)(2,1)}, bf16[7,2,128,128]{3,2,1,0:T(8,128)(2,1)S(1)}, bf16[7,2,128...) custom-call(s32[22]{0:T(128)S(1)} %concatenate.8.info, bf16[32,2,128,128]{3,2,1,0:T(8,128)(2,1)} %copy-done.1, ...), custom_call_target="tpu_custom_call" | custom-call | flops 11274289152 | bytes 16777216 | tf_op jit(solution)/shard_map/attention/pallas_call | solution.py:252
  108.9 7.8 %all-to-all-start.2 = ((bf16[32,2,128,128]{3,2,1,0:T(8,128)(2,1)}), bf16[32,2,128,128]{3,2,1,0:T(8,128)(2,1)}, u32[]{:S(2)}, u32[]{:S(2)}) async-start(bf16[32,2,128,128]{3,2,1,0:T(8,128)(2,1)} %get-tuple-element.9), calls=%async_computation.2 | async-start | bytes 4194304 | tf_op jit(solution)/shard_map/all_to_all | solution.py:337
  116.8 4.7 %collective-permute-start.6 = (bf16[6,2,128,128]{3,2,1,0:T(8,128)(2,1)S(1)}, bf16[6,2,128,128]{3,2,1,0:T(8,128)(2,1)S(1)}, u32[]{:S(2)}, u32[]{:S(2)}) collective-permute-start(bf16[6,2,128,128]{3,2,1,0:T(8,128)(2,1)S(1)} %get-tuple-element.13), channel_id=1, source_target_pairs={{0,32},{32,0},{64,96},{96,64},{1,33},{33,1},{65,97},{97,65},{2,34}... | collective-permute-start | bytes 1179656 | tf_op jit(solution)/shard_map/ppermute | solution.py:376
  121.4 1.3 collective-permute-start.4
  122.7 4.0 %collective-permute-start.5 = (bf16[7,2,128,128]{3,2,1,0:T(8,128)(2,1)S(1)}, bf16[7,2,128,128]{3,2,1,0:T(8,128)(2,1)S(1)}, u32[]{:S(2)}, u32[]{:S(2)}) collective-permute-start(bf16[7,2,128,128]{3,2,1,0:T(8,128)(2,1)S(1)} %get-tuple-element.12), channel_id=1, source_target_pairs={{0,32},{32,64},{64,96},{1,33},{33,65},{65,97},{2,34},{34,66},{66,9... | collective-permute-start | bytes 1376264 | tf_op jit(solution)/shard_map/ppermute | solution.py:375
  126.8 4.0 %collective-permute-done.6 = bf16[6,2,128,128]{3,2,1,0:T(8,128)(2,1)S(1)} collective-permute-done((bf16[6,2,128,128]{3,2,1,0:T(8,128)(2,1)S(1)}, bf16[6,2,128,128]{3,2,1,0:T(8,128)(2,1)S(1)}, u32[]{:S(2)}, u32[]{:S(2)}) %collective-permute-start.6) | collective-permute-done | bytes 393248 | tf_op jit(solution)/shard_map/ppermute | solution.py:376
  130.8 0.1 add_convert_fusion.glob_one
  130.9 1.2 collective-permute-start.7
  132.1 8.5 %collective-permute-done.4.back_a = bf16[7,2,128,128]{3,2,1,0:T(8,128)(2,1)S(1)} collective-permute-done((bf16[7,2,128,128]{3,2,1,0:T(8,128)(2,1)S(1)}, bf16[7,2,128,128]{3,2,1,0:T(8,128)(2,1)S(1)}, u32[]{:S(2)}, u32[]{:S(2)}) %collective-permute-start.4) | collective-permute-done | bytes 458784 | tf_op jit(solution)/shard_map/ppermute | solution.py:374
  140.6 1.2 collective-permute-done.7.glob_two
  141.8 2.4 %finish.1 = bf16[32,2,128,128]{3,2,1,0:T(8,128)(2,1)} custom-call(s32[22]{0:T(128)S(1)} %concatenate.8.info, bf16[32,2,128,128]{3,2,1,0:T(8,128)(2,1)S(1)} %copy-done, bf16[7,2,128,128]{3,2,1,0:T(8,128)(2,1)S(1)} %collective-permute-done.4.back_a, bf16[7,2,128,128]{3,2,1,0:T(8,128)(2,1)S(1)} %collective-permute-done.5.back_b, ...), custom_call_target="tpu_custom_call" | custom-call | flops 2097152 | bytes 6291456 | tf_op jit(solution)/shard_map/finish/pallas_call | solution.py:313
  144.2 1.0 all-to-all-done.2
  145.1 7.9 %all-to-all-start.3 = ((bf16[32,2,128,128]{3,2,1,0:T(8,128)(2,1)}), bf16[32,2,128,128]{3,2,1,0:T(8,128)(2,1)S(1)}, u32[]{:S(2)}, u32[]{:S(2)}) async-start(bf16[32,2,128,128]{3,2,1,0:T(8,128)(2,1)} %finish.1), calls=%async_computation.3 | async-start | bytes 4194304 | tf_op jit(solution)/shard_map/all_to_all | solution.py:337
  153.1 1.7 fusion.3
  154.8 2.0 %copy.23 = bf16[1,128,16,2,128]{4,3,2,1,0:T(2,128)(2,1)} copy(bf16[1,128,16,2,128]{4,1,0,2,3:T(8,128)(2,1)S(1)} %get-tuple-element.20) | data formatting | bytes 2097152 | tf_op jit(solution)/shard_map/slice | solution.py:333
  156.8 2.0 %copy.22 = bf16[1,128,16,2,128]{4,3,2,1,0:T(2,128)(2,1)} copy(bf16[1,128,16,2,128]{4,1,0,2,3:T(8,128)(2,1)S(1)} %get-tuple-element.21) | data formatting | bytes 2097152 | tf_op jit(solution)/shard_map/slice | solution.py:333
  158.9 22.5 %all-to-all-done.3 = bf16[32,2,128,128]{3,2,1,0:T(8,128)(2,1)S(1)} async-done(((bf16[32,2,128,128]{3,2,1,0:T(8,128)(2,1)}), bf16[32,2,128,128]{3,2,1,0:T(8,128)(2,1)S(1)}, u32[]{:S(2)}, u32[]{:S(2)}) %all-to-all-start.3) | async-done | bytes 2097184 | tf_op jit(solution)/shard_map/all_to_all | solution.py:337
  181.4 0.1 fusion.2
  181.5 2.0 %copy.25 = bf16[1,128,16,2,128]{4,3,2,1,0:T(2,128)(2,1)} copy(bf16[1,128,16,2,128]{4,1,0,2,3:T(8,128)(2,1)S(1)} %get-tuple-element.18) | data formatting | bytes 2097152 | tf_op jit(solution)/shard_map/slice | solution.py:333
  183.6 2.0 %copy.24 = bf16[1,128,16,2,128]{4,3,2,1,0:T(2,128)(2,1)} copy(bf16[1,128,16,2,128]{4,1,0,2,3:T(8,128)(2,1)S(1)} %get-tuple-element.19) | data formatting | bytes 2097152 | tf_op jit(solution)/shard_map/slice | solution.py:333
  (22 shorter events, 0.2 us)
Async XLA Ops:
  0.6 1.7 copy-start.2
  4.3 9.6 %copy-start.6 = (s32[6]{0:T(128)S(1)}, s32[6]{0:T(128)}, u32[]{:S(2)}) copy-start(s32[6]{0:T(128)} %param.11) | copy-start | bytes 76
  4.3 37.9 %all-to-all-start = ((bf16[32,2,128,128]{3,2,1,0:T(8,128)(2,1)}), bf16[32,2,128,128]{3,2,1,0:T(8,128)(2,1)S(1)}, u32[]{:S(2)}, u32[]{:S(2)}) async-start(bf16[32,2,128,128]{3,2,1,0:T(8,128)(2,1)} %bitcast.9), calls=%async_computation | async-start | bytes 4194304 | tf_op jit(solution)/shard_map/all_to_all | solution.py:337
  42.2 18.8 %copy-start.1 = (bf16[32,2,128,128]{3,2,1,0:T(8,128)(2,1)}, bf16[32,2,128,128]{3,2,1,0:T(8,128)(2,1)S(1)}, u32[]{:S(2)}) copy-start(bf16[32,2,128,128]{3,2,1,0:T(8,128)(2,1)S(1)} %all-to-all-done.kv) | copy-start | bytes 6291460
  42.2 33.6 %all-to-all-start.1 = ((bf16[32,2,128,128]{3,2,1,0:T(8,128)(2,1)}), bf16[32,2,128,128]{3,2,1,0:T(8,128)(2,1)}, u32[]{:S(2)}, u32[]{:S(2)}) async-start(bf16[32,2,128,128]{3,2,1,0:T(8,128)(2,1)} %bitcast.13), calls=%async_computation.1 | async-start | bytes 4194304 | tf_op jit(solution)/shard_map/all_to_all | solution.py:337
  47.4 19.0 %copy-start.3 = (s32[2]{0:T(128)S(1)}, s32[2]{0:T(128)}, u32[]{:S(2)}) copy-start(s32[2]{0:T(128)} %param.10) | copy-start | bytes 28
  47.6 10.5 %collective-permute-start.2 = (bf16[6,2,128,128]{3,2,1,0:T(8,128)(2,1)S(1)}, bf16[6,2,128,128]{3,2,1,0:T(8,128)(2,1)S(1)}, u32[]{:S(2)}, u32[]{:S(2)}) collective-permute-start(bf16[6,2,128,128]{3,2,1,0:T(8,128)(2,1)S(1)} %dynamic-slice_dynamic-update-slice_fusion), channel_id=1, source_target_pairs={{0,32},{32,0},{64,96},{96,64},{1,33},{33,1},{65,97},{97,65},{2,34}... | collective-permute-start | bytes 1179656 | tf_op jit(solution)/shard_map/ppermute | solution.py:366
  58.1 11.0 %collective-permute-start.3 = (bf16[6,2,128,128]{3,2,1,0:T(8,128)(2,1)S(1)}, bf16[6,2,128,128]{3,2,1,0:T(8,128)(2,1)}, u32[]{:S(2)}, u32[]{:S(2)}) collective-permute-start(bf16[6,2,128,128]{3,2,1,0:T(8,128)(2,1)S(1)} %broadcast_select_fusion), channel_id=1, source_target_pairs={{32,64},{64,32},{96,0},{0,96},{33,65},{65,33},{97,1},{1,97},{34,66... | collective-permute-start | bytes 1179656 | tf_op jit(solution)/shard_map/ppermute | solution.py:368
  61.0 14.8 %collective-permute-start.1 = (bf16[7,2,128,128]{3,2,1,0:T(8,128)(2,1)S(1)}, bf16[7,2,128,128]{3,2,1,0:T(8,128)(2,1)S(1)}, u32[]{:S(2)}, u32[]{:S(2)}) collective-permute-start(bf16[7,2,128,128]{3,2,1,0:T(8,128)(2,1)S(1)} %get-tuple-element.22), channel_id=1, source_target_pairs={{96,64},{64,32},{32,0},{97,65},{65,33},{33,1},{98,66},{66,34},{34,... | collective-permute-start | bytes 1376264 | tf_op jit(solution)/shard_map/ppermute | solution.py:364
  62.3 13.5 %collective-permute-start = (bf16[7,2,128,128]{3,2,1,0:T(8,128)(2,1)S(1)}, bf16[7,2,128,128]{3,2,1,0:T(8,128)(2,1)S(1)}, u32[]{:S(2)}, u32[]{:S(2)}) collective-permute-start(bf16[7,2,128,128]{3,2,1,0:T(8,128)(2,1)S(1)} %get-tuple-element.23), channel_id=1, source_target_pairs={{0,32},{32,64},{64,96},{1,33},{33,65},{65,97},{2,34},{34,66},{66,9... | collective-permute-start | bytes 1376264 | tf_op jit(solution)/shard_map/ppermute | solution.py:363
  75.8 0.8 copy-start.4
  76.6 0.8 copy-start.5
  108.9 32.9 %copy-start = (bf16[32,2,128,128]{3,2,1,0:T(8,128)(2,1)S(1)}, bf16[32,2,128,128]{3,2,1,0:T(8,128)(2,1)}, u32[]{:S(2)}) copy-start(bf16[32,2,128,128]{3,2,1,0:T(8,128)(2,1)} %get-tuple-element.10.own) | copy-start | bytes 6291460
  108.9 36.2 %all-to-all-start.2 = ((bf16[32,2,128,128]{3,2,1,0:T(8,128)(2,1)}), bf16[32,2,128,128]{3,2,1,0:T(8,128)(2,1)}, u32[]{:S(2)}, u32[]{:S(2)}) async-start(bf16[32,2,128,128]{3,2,1,0:T(8,128)(2,1)} %get-tuple-element.9), calls=%async_computation.2 | async-start | bytes 4194304 | tf_op jit(solution)/shard_map/all_to_all | solution.py:337
  116.8 14.0 %collective-permute-start.6 = (bf16[6,2,128,128]{3,2,1,0:T(8,128)(2,1)S(1)}, bf16[6,2,128,128]{3,2,1,0:T(8,128)(2,1)S(1)}, u32[]{:S(2)}, u32[]{:S(2)}) collective-permute-start(bf16[6,2,128,128]{3,2,1,0:T(8,128)(2,1)S(1)} %get-tuple-element.13), channel_id=1, source_target_pairs={{0,32},{32,0},{64,96},{96,64},{1,33},{33,1},{65,97},{97,65},{2,34}... | collective-permute-start | bytes 1179656 | tf_op jit(solution)/shard_map/ppermute | solution.py:376
  121.4 19.2 %collective-permute-start.4 = (bf16[7,2,128,128]{3,2,1,0:T(8,128)(2,1)S(1)}, bf16[7,2,128,128]{3,2,1,0:T(8,128)(2,1)S(1)}, u32[]{:S(2)}, u32[]{:S(2)}) collective-permute-start(bf16[7,2,128,128]{3,2,1,0:T(8,128)(2,1)S(1)} %get-tuple-element.11), channel_id=1, source_target_pairs={{32,0},{64,32},{96,64},{33,1},{65,33},{97,65},{34,2},{66,34},{98,6... | collective-permute-start | bytes 1376264 | tf_op jit(solution)/shard_map/ppermute | solution.py:374
  122.7 17.9 %collective-permute-start.5 = (bf16[7,2,128,128]{3,2,1,0:T(8,128)(2,1)S(1)}, bf16[7,2,128,128]{3,2,1,0:T(8,128)(2,1)S(1)}, u32[]{:S(2)}, u32[]{:S(2)}) collective-permute-start(bf16[7,2,128,128]{3,2,1,0:T(8,128)(2,1)S(1)} %get-tuple-element.12), channel_id=1, source_target_pairs={{0,32},{32,64},{64,96},{1,33},{33,65},{65,97},{2,34},{34,66},{66,9... | collective-permute-start | bytes 1376264 | tf_op jit(solution)/shard_map/ppermute | solution.py:375
  130.9 10.9 %collective-permute-start.7 = (bf16[6,2,128,128]{3,2,1,0:T(8,128)(2,1)S(1)}, bf16[6,2,128,128]{3,2,1,0:T(8,128)(2,1)S(1)}, u32[]{:S(2)}, u32[]{:S(2)}) collective-permute-start(bf16[6,2,128,128]{3,2,1,0:T(8,128)(2,1)S(1)} %add_convert_fusion.glob_one), channel_id=1, source_target_pairs={{32,64},{64,32},{96,0},{0,96},{33,65},{65,33},{97,1},{1,97},{34,66... | collective-permute-start | bytes 1179656 | tf_op jit(solution)/shard_map/ppermute | solution.py:378
  145.1 36.3 %all-to-all-start.3 = ((bf16[32,2,128,128]{3,2,1,0:T(8,128)(2,1)}), bf16[32,2,128,128]{3,2,1,0:T(8,128)(2,1)S(1)}, u32[]{:S(2)}, u32[]{:S(2)}) async-start(bf16[32,2,128,128]{3,2,1,0:T(8,128)(2,1)} %finish.1), calls=%async_computation.3 | async-start | bytes 4194304 | tf_op jit(solution)/shard_map/all_to_all | solution.py:337
where the time goes:
time: 188 us; the launch traced here: 186 us
  waiting for transfers between devices  61.4 us (33%)
  starting transfers between devices  51.2 us (27%)
  Pallas kernels  33.9 us (18%)
  local copies, waits for them, and re-layouts  19.4 us (10%)
  between operations  13.6 us (7%)
  other arithmetic  5.97 us (3%)
    all_to_all x4, waiting for transfers between devices, exchange(): return lax.all_to_all(x, GROUP, 0, 0, tiled=True)  37.9 us
    pallas_call x1, Pallas kernels, attention(): pl.pallas_call(attention_kernel, out_shape=(sds((32, 2, BLK, HD), BF16),...  31.6 us
    all_to_all x4, starting transfers between devices, exchange(): return lax.all_to_all(x, GROUP, 0, 0, tiled=True)  30.6 us
    slice x6, local copies, waits for them, and re-layouts, to_rows(): return (pair[0], pair[1])  10 us
    ppermute x1, waiting for transfers between devices, shards(): other = lax.ppermute(mine, 'y', PAIR_ONE)  9.04 us
    ppermute x1, waiting for transfers between devices, shards(): back_a = lax.ppermute(back_a, 'y', [(1, 0), (2, 1), (3, 2)])  8.5 us
    another operation x4, local copies, waits for them, and re-layouts, to_heads(): pair = jnp.stack([x, y], axis=0).reshape(2, BLK, 16, 2, HD)  6.37 us
    ppermute x1, starting transfers between devices, shards(): other = lax.ppermute(glob_grad, 'y', PAIR_ONE)  4.66 us
  transfers between devices with their start and end apart: 12, of which 9 were waited for; matrix products, arithmetic and copies ran while one was open for 9% of the time, Pallas kernels for 1%

commit v1 on v0

--- a/solution.py
+++ b/solution.py
@@ -364,6 +364,7 @@
     halo_b = lax.ppermute(kv[9:16], "y", [(3, 2), (2, 1), (1, 0)])
     mine = jnp.concatenate([lax.dynamic_slice_in_dim(kv, where[s], 1, 0) for s in range(GLOB)], axis=0)
     other = lax.ppermute(mine, "y", PAIR_ONE)
+    halo_a, halo_b, other = lax.optimization_barrier((halo_a, halo_b, other))
     mine = jnp.where((owner == me)[:, None, None, None], mine, other)
     other = lax.ppermute(mine, "y", PAIR_TWO)
     glob = jnp.where((owner // 2 == me // 2)[:, None, None, None], mine, other)

time: 188 us -> 194 us (1.032)
  waiting for transfers between devices: 61.4 us -> 70.1 us
    ppermute x1, waiting for transfers between devices: 9.04 us -> 16 us  [shards(): other = lax.ppermute(mine, 'y', PAIR_ONE)]
    ppermute x1, waiting for transfers between devices: 0.76 us -> 5.98 us  [shards(): other = lax.ppermute(mine, 'y', PAIR_TWO)]
    ppermute x1, starting transfers between devices: 4.66 us -> 0.09 us  [shards(): other = lax.ppermute(glob_grad, 'y', PAIR_ONE)]
    all_to_all x4, waiting for transfers between devices: 37.9 us -> 35.2 us  [exchange(): return lax.all_to_all(x, GROUP, 0, 0, tiled=True)]
    ppermute x1, waiting for transfers between devices: 8.5 us -> 6.02 us  [shards(): back_a = lax.ppermute(back_a, 'y', [(1, 0), (2, 1), (3, 2)])]
    ppermute x1, starting transfers between devices: 1.22 us -> 3.69 us  [shards(): other = lax.ppermute(glob_grad, 'y', PAIR_TWO)]
  transfers between devices with their start and end apart: 12 -> 12, of which waited for: 9 -> 8; matrix products, arithmetic and copies ran while one was open for 9% -> 8% of each run, Pallas kernels for 1% -> 1%
where the time goes in v1:
time: 194 us; the launch traced here: 190 us
  waiting for transfers between devices  70.1 us (36%)
  starting transfers between devices  50.5 us (26%)
  Pallas kernels  32.6 us (17%)
  local copies, waits for them, and re-layouts  18.5 us (10%)
  between operations  13.7 us (7%)
  other arithmetic  5 us (3%)
    all_to_all x4, waiting for transfers between devices, exchange(): return lax.all_to_all(x, GROUP, 0, 0, tiled=True)  35.2 us
    all_to_all x4, starting transfers between devices, exchange(): return lax.all_to_all(x, GROUP, 0, 0, tiled=True)  30.7 us
    pallas_call x1, Pallas kernels, attention(): pl.pallas_call(attention_kernel, out_shape=(sds((32, 2, BLK, HD), BF16),...  30.3 us
    ppermute x1, waiting for transfers between devices, shards(): other = lax.ppermute(mine, 'y', PAIR_ONE)  16 us
    slice x6, local copies, waits for them, and re-layouts, to_rows(): return (pair[0], pair[1])  10 us
    another operation x4, local copies, waits for them, and re-layouts, to_heads(): pair = jnp.stack([x, y], axis=0).reshape(2, BLK, 16, 2, HD)  6.37 us
    ppermute x1, waiting for transfers between devices, shards(): back_a = lax.ppermute(back_a, 'y', [(1, 0), (2, 1), (3, 2)])  6.02 us
    ppermute x1, waiting for transfers between devices, shards(): other = lax.ppermute(mine, 'y', PAIR_TWO)  5.98 us
  transfers between devices with their start and end apart: 12, of which 8 were waited for; matrix products, arithmetic and copies ran while one was open for 8% of the time, Pallas kernels for 1%

profile of v1, /device:TPU:1, one launch (start us, length us, event | category | flops | bytes accessed | tf_op | source)
XLA Modules:
  0.0 190.4 jit_solution(724144505918316320)
XLA Ops:
  0.6 1.7 copy.18
  2.4 0.4 copy.19
  2.8 1.5 pad_maximum_fusion
  4.3 9.6 %all-to-all-start = ((bf16[32,2,128,128]{3,2,1,0:T(8,128)(2,1)}), bf16[32,2,128,128]{3,2,1,0:T(8,128)(2,1)S(1)}, u32[]{:S(2)}, u32[]{:S(2)}) async-start(bf16[32,2,128,128]{3,2,1,0:T(8,128)(2,1)} %bitcast.9), calls=%async_computation | async-start | bytes 4194304 | tf_op jit(solution)/shard_map/all_to_all | solution.py:337
  13.9 0.2 convert_reduce_fusion
  14.1 0.1 select_reduce_fusion
  14.2 0.6 fusion.5
  22.5 1.6 copy.20
  24.1 2.6 %copy.21 = bf16[1,128,16,2,128]{4,1,0,2,3:T(8,128)(2,1)} copy(bf16[1,128,16,2,128]{4,3,2,1,0:T(2,128)(2,1)} %bitcast.36) | data formatting | bytes 2097152 | tf_op jit(solution)/shard_map/stack | solution.py:325
  30.6 2.8 %pad_maximum_fusion.1 = bf16[2,128,16,2,128]{4,1,0,2,3:T(8,128)(2,1)} fusion(bf16[1,128,16,2,128]{4,1,0,2,3:T(8,128)(2,1)} %copy.21, bf16[1,128,16,2,128]{4,1,0,2,3:T(8,128)(2,1)S(1)} %copy.20), kind=kLoop, calls=%fused_computation.1 | loop fusion | flops 1048576 | bytes 4194304 | tf_op jit(solution)/shard_map/stack | solution.py:325
  33.4 8.8 %all-to-all-done.kv = bf16[32,2,128,128]{3,2,1,0:T(8,128)(2,1)S(1)} async-done(((bf16[32,2,128,128]{3,2,1,0:T(8,128)(2,1)}), bf16[32,2,128,128]{3,2,1,0:T(8,128)(2,1)S(1)}, u32[]{:S(2)}, u32[]{:S(2)}) %all-to-all-start) | async-done | bytes 2097184 | tf_op jit(solution)/shard_map/all_to_all | solution.py:337
  42.2 5.2 %all-to-all-start.1 = ((bf16[32,2,128,128]{3,2,1,0:T(8,128)(2,1)}), bf16[32,2,128,128]{3,2,1,0:T(8,128)(2,1)}, u32[]{:S(2)}, u32[]{:S(2)}) async-start(bf16[32,2,128,128]{3,2,1,0:T(8,128)(2,1)} %bitcast.13), calls=%async_computation.1 | async-start | bytes 4194304 | tf_op jit(solution)/shard_map/all_to_all | solution.py:337
  47.4 0.0 copy-start.3
  47.4 0.1 fusion.4
  47.5 1.3 collective-permute-start.1
  48.8 4.0 %collective-permute-start = (bf16[7,2,128,128]{3,2,1,0:T(8,128)(2,1)S(1)}, bf16[7,2,128,128]{3,2,1,0:T(8,128)(2,1)S(1)}, u32[]{:S(2)}, u32[]{:S(2)}) collective-permute-start(bf16[7,2,128,128]{3,2,1,0:T(8,128)(2,1)S(1)} %get-tuple-element.29), channel_id=1, source_target_pairs={{0,32},{32,64},{64,96},{1,33},{33,65},{65,97},{2,34},{34,66},{66,9... | collective-permute-start | bytes 1376264 | tf_op jit(solution)/shard_map/ppermute | solution.py:363
  53.0 1.4 collective-permute-start.2
  54.3 16.0 %collective-permute-done.2 = bf16[6,2,128,128]{3,2,1,0:T(8,128)(2,1)S(1)} collective-permute-done((bf16[6,2,128,128]{3,2,1,0:T(8,128)(2,1)S(1)}, bf16[6,2,128,128]{3,2,1,0:T(8,128)(2,1)S(1)}, u32[]{:S(2)}, u32[]{:S(2)}) %collective-permute-start.2) | collective-permute-done | bytes 393248 | tf_op jit(solution)/shard_map/ppermute | solution.py:366
  70.3 0.0 collective-permute-done.1.halo_b
  70.3 0.0 collective-permute-done.halo_a
  70.3 0.1 broadcast_select_fusion
  70.5 0.6 copy-done.4
  71.1 4.1 %collective-permute-start.3 = (bf16[6,2,128,128]{3,2,1,0:T(8,128)(2,1)S(1)}, bf16[6,2,128,128]{3,2,1,0:T(8,128)(2,1)S(1)}, u32[]{:S(2)}, u32[]{:S(2)}) collective-permute-start(bf16[6,2,128,128]{3,2,1,0:T(8,128)(2,1)S(1)} %broadcast_select_fusion), channel_id=1, source_target_pairs={{32,64},{64,32},{96,0},{0,96},{33,65},{65,33},{97,1},{1,97},{34,66... | collective-permute-start | bytes 1179656 | tf_op jit(solution)/shard_map/ppermute | solution.py:369
  75.2 0.6 fusion.6
  77.1 0.1 concatenate.8.info
  77.1 6.0 %collective-permute-done.3 = bf16[6,2,128,128]{3,2,1,0:T(8,128)(2,1)S(1)} collective-permute-done((bf16[6,2,128,128]{3,2,1,0:T(8,128)(2,1)S(1)}, bf16[6,2,128,128]{3,2,1,0:T(8,128)(2,1)S(1)}, u32[]{:S(2)}, u32[]{:S(2)}) %collective-permute-start.3) | collective-permute-done | bytes 393248 | tf_op jit(solution)/shard_map/ppermute | solution.py:369
  83.1 0.1 broadcast_select_fusion.1.glob
  83.3 0.0 all-to-all-done.1.qd
  83.3 30.3 %attention.1 = (bf16[32,2,128,128]{3,2,1,0:T(8,128)(2,1)}, bf16[32,2,128,128]{3,2,1,0:T(8,128)(2,1)}, bf16[7,2,128,128]{3,2,1,0:T(8,128)(2,1)S(1)}, bf16[7,2,128...) custom-call(s32[22]{0:T(128)S(1)} %concatenate.8.info, bf16[32,2,128,128]{3,2,1,0:T(8,128)(2,1)} %copy-done.1, ...), custom_call_target="tpu_custom_call" | custom-call | flops 11274289152 | bytes 16777216 | tf_op jit(solution)/shard_map/attention/pallas_call | solution.py:252
  113.5 10.6 %all-to-all-start.2 = ((bf16[32,2,128,128]{3,2,1,0:T(8,128)(2,1)}), bf16[32,2,128,128]{3,2,1,0:T(8,128)(2,1)}, u32[]{:S(2)}, u32[]{:S(2)}) async-start(bf16[32,2,128,128]{3,2,1,0:T(8,128)(2,1)} %get-tuple-element.15), calls=%async_computation.2 | async-start | bytes 4194304 | tf_op jit(solution)/shard_map/all_to_all | solution.py:337
  124.1 0.1 collective-permute-start.6
  124.2 1.3 collective-permute-start.4
  125.5 4.0 %collective-permute-start.5 = (bf16[7,2,128,128]{3,2,1,0:T(8,128)(2,1)S(1)}, bf16[7,2,128,128]{3,2,1,0:T(8,128)(2,1)S(1)}, u32[]{:S(2)}, u32[]{:S(2)}) collective-permute-start(bf16[7,2,128,128]{3,2,1,0:T(8,128)(2,1)S(1)} %get-tuple-element.18), channel_id=1, source_target_pairs={{0,32},{32,64},{64,96},{1,33},{33,65},{65,97},{2,34},{34,66},{66,9... | collective-permute-start | bytes 1376264 | tf_op jit(solution)/shard_map/ppermute | solution.py:376
  129.5 5.2 %collective-permute-done.6 = bf16[6,2,128,128]{3,2,1,0:T(8,128)(2,1)S(1)} collective-permute-done((bf16[6,2,128,128]{3,2,1,0:T(8,128)(2,1)S(1)}, bf16[6,2,128,128]{3,2,1,0:T(8,128)(2,1)S(1)}, u32[]{:S(2)}, u32[]{:S(2)}) %collective-permute-start.6) | collective-permute-done | bytes 393248 | tf_op jit(solution)/shard_map/ppermute | solution.py:377
  134.7 0.1 add_convert_fusion.glob_one
  134.8 3.7 %collective-permute-start.7 = (bf16[6,2,128,128]{3,2,1,0:T(8,128)(2,1)S(1)}, bf16[6,2,128,128]{3,2,1,0:T(8,128)(2,1)S(1)}, u32[]{:S(2)}, u32[]{:S(2)}) collective-permute-start(bf16[6,2,128,128]{3,2,1,0:T(8,128)(2,1)S(1)} %add_convert_fusion.glob_one), channel_id=1, source_target_pairs={{32,64},{64,32},{96,0},{0,96},{33,65},{65,33},{97,1},{1,97},{34,66... | collective-permute-start | bytes 1179656 | tf_op jit(solution)/shard_map/ppermute | solution.py:379
  138.5 6.0 %collective-permute-done.4.back_a = bf16[7,2,128,128]{3,2,1,0:T(8,128)(2,1)S(1)} collective-permute-done((bf16[7,2,128,128]{3,2,1,0:T(8,128)(2,1)S(1)}, bf16[7,2,128,128]{3,2,1,0:T(8,128)(2,1)S(1)}, u32[]{:S(2)}, u32[]{:S(2)}) %collective-permute-start.4) | collective-permute-done | bytes 458784 | tf_op jit(solution)/shard_map/ppermute | solution.py:375
  144.5 1.7 collective-permute-done.7.glob_two
  146.3 2.3 %finish.1 = bf16[32,2,128,128]{3,2,1,0:T(8,128)(2,1)} custom-call(s32[22]{0:T(128)S(1)} %concatenate.8.info, bf16[32,2,128,128]{3,2,1,0:T(8,128)(2,1)S(1)} %copy-done, bf16[7,2,128,128]{3,2,1,0:T(8,128)(2,1)S(1)} %collective-permute-done.4.back_a, bf16[7,2,128,128]{3,2,1,0:T(8,128)(2,1)S(1)} %collective-permute-done.5.back_b, ...), custom_call_target="tpu_custom_call" | custom-call | flops 2097152 | bytes 6291456 | tf_op jit(solution)/shard_map/finish/pallas_call | solution.py:313
  148.6 3.9 %all-to-all-done.2 = bf16[32,2,128,128]{3,2,1,0:T(8,128)(2,1)} async-done(((bf16[32,2,128,128]{3,2,1,0:T(8,128)(2,1)}), bf16[32,2,128,128]{3,2,1,0:T(8,128)(2,1)}, u32[]{:S(2)}, u32[]{:S(2)}) %all-to-all-start.2) | async-done | bytes 2097184 | tf_op jit(solution)/shard_map/all_to_all | solution.py:337
  152.5 5.4 %all-to-all-start.3 = ((bf16[32,2,128,128]{3,2,1,0:T(8,128)(2,1)}), bf16[32,2,128,128]{3,2,1,0:T(8,128)(2,1)S(1)}, u32[]{:S(2)}, u32[]{:S(2)}) async-start(bf16[32,2,128,128]{3,2,1,0:T(8,128)(2,1)} %finish.1), calls=%async_computation.3 | async-start | bytes 4194304 | tf_op jit(solution)/shard_map/all_to_all | solution.py:337
  157.9 1.7 fusion.3
  159.6 2.0 %copy.23 = bf16[1,128,16,2,128]{4,3,2,1,0:T(2,128)(2,1)} copy(bf16[1,128,16,2,128]{4,1,0,2,3:T(8,128)(2,1)S(1)} %get-tuple-element.26) | data formatting | bytes 2097152 | tf_op jit(solution)/shard_map/slice | solution.py:333
  161.6 2.0 %copy.22 = bf16[1,128,16,2,128]{4,3,2,1,0:T(2,128)(2,1)} copy(bf16[1,128,16,2,128]{4,1,0,2,3:T(8,128)(2,1)S(1)} %get-tuple-element.27) | data formatting | bytes 2097152 | tf_op jit(solution)/shard_map/slice | solution.py:333
  163.6 22.5 %all-to-all-done.3 = bf16[32,2,128,128]{3,2,1,0:T(8,128)(2,1)S(1)} async-done(((bf16[32,2,128,128]{3,2,1,0:T(8,128)(2,1)}), bf16[32,2,128,128]{3,2,1,0:T(8,128)(2,1)S(1)}, u32[]{:S(2)}, u32[]{:S(2)}) %all-to-all-start.3) | async-done | bytes 2097184 | tf_op jit(solution)/shard_map/all_to_all | solution.py:337
  186.2 0.1 fusion.2
  186.3 2.0 %copy.25 = bf16[1,128,16,2,128]{4,3,2,1,0:T(2,128)(2,1)} copy(bf16[1,128,16,2,128]{4,1,0,2,3:T(8,128)(2,1)S(1)} %get-tuple-element.24) | data formatting | bytes 2097152 | tf_op jit(solution)/shard_map/slice | solution.py:333
  188.3 2.0 %copy.24 = bf16[1,128,16,2,128]{4,3,2,1,0:T(2,128)(2,1)} copy(bf16[1,128,16,2,128]{4,1,0,2,3:T(8,128)(2,1)S(1)} %get-tuple-element.25) | data formatting | bytes 2097152 | tf_op jit(solution)/shard_map/slice | solution.py:333
  (22 shorter events, 0.2 us)
Async XLA Ops:
  0.6 1.7 copy-start.2
  4.3 9.6 %copy-start.6 = (s32[6]{0:T(128)S(1)}, s32[6]{0:T(128)}, u32[]{:S(2)}) copy-start(s32[6]{0:T(128)} %param.11) | copy-start | bytes 76
  4.3 37.9 %all-to-all-start = ((bf16[32,2,128,128]{3,2,1,0:T(8,128)(2,1)}), bf16[32,2,128,128]{3,2,1,0:T(8,128)(2,1)S(1)}, u32[]{:S(2)}, u32[]{:S(2)}) async-start(bf16[32,2,128,128]{3,2,1,0:T(8,128)(2,1)} %bitcast.9), calls=%async_computation | async-start | bytes 4194304 | tf_op jit(solution)/shard_map/all_to_all | solution.py:337
  42.2 10.7 %copy-start.1 = (bf16[32,2,128,128]{3,2,1,0:T(8,128)(2,1)}, bf16[32,2,128,128]{3,2,1,0:T(8,128)(2,1)S(1)}, u32[]{:S(2)}) copy-start(bf16[32,2,128,128]{3,2,1,0:T(8,128)(2,1)S(1)} %all-to-all-done.kv) | copy-start | bytes 6291460
  42.2 41.1 %all-to-all-start.1 = ((bf16[32,2,128,128]{3,2,1,0:T(8,128)(2,1)}), bf16[32,2,128,128]{3,2,1,0:T(8,128)(2,1)}, u32[]{:S(2)}, u32[]{:S(2)}) async-start(bf16[32,2,128,128]{3,2,1,0:T(8,128)(2,1)} %bitcast.13), calls=%async_computation.1 | async-start | bytes 4194304 | tf_op jit(solution)/shard_map/all_to_all | solution.py:337
  47.4 27.8 %copy-start.3 = (s32[2]{0:T(128)S(1)}, s32[2]{0:T(128)}, u32[]{:S(2)}) copy-start(s32[2]{0:T(128)} %param.10) | copy-start | bytes 28
  47.5 22.9 %collective-permute-start.1 = (bf16[7,2,128,128]{3,2,1,0:T(8,128)(2,1)S(1)}, bf16[7,2,128,128]{3,2,1,0:T(8,128)(2,1)S(1)}, u32[]{:S(2)}, u32[]{:S(2)}) collective-permute-start(bf16[7,2,128,128]{3,2,1,0:T(8,128)(2,1)S(1)} %get-tuple-element.28), channel_id=1, source_target_pairs={{96,64},{64,32},{32,0},{97,65},{65,33},{33,1},{98,66},{66,34},{34,... | collective-permute-start | bytes 1376264 | tf_op jit(solution)/shard_map/ppermute | solution.py:364
  48.8 21.6 %collective-permute-start = (bf16[7,2,128,128]{3,2,1,0:T(8,128)(2,1)S(1)}, bf16[7,2,128,128]{3,2,1,0:T(8,128)(2,1)S(1)}, u32[]{:S(2)}, u32[]{:S(2)}) collective-permute-start(bf16[7,2,128,128]{3,2,1,0:T(8,128)(2,1)S(1)} %get-tuple-element.29), channel_id=1, source_target_pairs={{0,32},{32,64},{64,96},{1,33},{33,65},{65,97},{2,34},{34,66},{66,9... | collective-permute-start | bytes 1376264 | tf_op jit(solution)/shard_map/ppermute | solution.py:363
  53.0 17.4 %collective-permute-start.2 = (bf16[6,2,128,128]{3,2,1,0:T(8,128)(2,1)S(1)}, bf16[6,2,128,128]{3,2,1,0:T(8,128)(2,1)S(1)}, u32[]{:S(2)}, u32[]{:S(2)}) collective-permute-start(bf16[6,2,128,128]{3,2,1,0:T(8,128)(2,1)S(1)} %dynamic-slice_dynamic-update-slice_fusion), channel_id=1, source_target_pairs={{0,32},{32,0},{64,96},{96,64},{1,33},{33,1},{65,97},{97,65},{2,34}... | collective-permute-start | bytes 1179656 | tf_op jit(solution)/shard_map/ppermute | solution.py:366
  70.3 0.8 copy-start.4
  70.3 12.9 %copy-start.5 = (bf16[7,2,128,128]{3,2,1,0:T(8,128)(2,1)}, bf16[7,2,128,128]{3,2,1,0:T(8,128)(2,1)S(1)}, u32[]{:S(2)}) copy-start(bf16[7,2,128,128]{3,2,1,0:T(8,128)(2,1)S(1)} %collective-permute-done.halo_a) | copy-start | bytes 1376260
  71.1 12.0 %collective-permute-start.3 = (bf16[6,2,128,128]{3,2,1,0:T(8,128)(2,1)S(1)}, bf16[6,2,128,128]{3,2,1,0:T(8,128)(2,1)S(1)}, u32[]{:S(2)}, u32[]{:S(2)}) collective-permute-start(bf16[6,2,128,128]{3,2,1,0:T(8,128)(2,1)S(1)} %broadcast_select_fusion), channel_id=1, source_target_pairs={{32,64},{64,32},{96,0},{0,96},{33,65},{65,33},{97,1},{1,97},{34,66... | collective-permute-start | bytes 1179656 | tf_op jit(solution)/shard_map/ppermute | solution.py:369
  113.5 32.7 %copy-start = (bf16[32,2,128,128]{3,2,1,0:T(8,128)(2,1)S(1)}, bf16[32,2,128,128]{3,2,1,0:T(8,128)(2,1)}, u32[]{:S(2)}) copy-start(bf16[32,2,128,128]{3,2,1,0:T(8,128)(2,1)} %get-tuple-element.16.own) | copy-start | bytes 6291460
  113.5 38.9 %all-to-all-start.2 = ((bf16[32,2,128,128]{3,2,1,0:T(8,128)(2,1)}), bf16[32,2,128,128]{3,2,1,0:T(8,128)(2,1)}, u32[]{:S(2)}, u32[]{:S(2)}) async-start(bf16[32,2,128,128]{3,2,1,0:T(8,128)(2,1)} %get-tuple-element.15), calls=%async_computation.2 | async-start | bytes 4194304 | tf_op jit(solution)/shard_map/all_to_all | solution.py:337
  124.1 10.6 %collective-permute-start.6 = (bf16[6,2,128,128]{3,2,1,0:T(8,128)(2,1)S(1)}, bf16[6,2,128,128]{3,2,1,0:T(8,128)(2,1)S(1)}, u32[]{:S(2)}, u32[]{:S(2)}) collective-permute-start(bf16[6,2,128,128]{3,2,1,0:T(8,128)(2,1)S(1)} %get-tuple-element.19), channel_id=1, source_target_pairs={{0,32},{32,0},{64,96},{96,64},{1,33},{33,1},{65,97},{97,65},{2,34}... | collective-permute-start | bytes 1179656 | tf_op jit(solution)/shard_map/ppermute | solution.py:377
  124.2 20.3 %collective-permute-start.4 = (bf16[7,2,128,128]{3,2,1,0:T(8,128)(2,1)S(1)}, bf16[7,2,128,128]{3,2,1,0:T(8,128)(2,1)S(1)}, u32[]{:S(2)}, u32[]{:S(2)}) collective-permute-start(bf16[7,2,128,128]{3,2,1,0:T(8,128)(2,1)S(1)} %get-tuple-element.17), channel_id=1, source_target_pairs={{32,0},{64,32},{96,64},{33,1},{65,33},{97,65},{34,2},{66,34},{98,6... | collective-permute-start | bytes 1376264 | tf_op jit(solution)/shard_map/ppermute | solution.py:375
  125.5 19.0 %collective-permute-start.5 = (bf16[7,2,128,128]{3,2,1,0:T(8,128)(2,1)S(1)}, bf16[7,2,128,128]{3,2,1,0:T(8,128)(2,1)S(1)}, u32[]{:S(2)}, u32[]{:S(2)}) collective-permute-start(bf16[7,2,128,128]{3,2,1,0:T(8,128)(2,1)S(1)} %get-tuple-element.18), channel_id=1, source_target_pairs={{0,32},{32,64},{64,96},{1,33},{33,65},{65,97},{2,34},{34,66},{66,9... | collective-permute-start | bytes 1376264 | tf_op jit(solution)/shard_map/ppermute | solution.py:376
  134.8 11.5 %collective-permute-start.7 = (bf16[6,2,128,128]{3,2,1,0:T(8,128)(2,1)S(1)}, bf16[6,2,128,128]{3,2,1,0:T(8,128)(2,1)S(1)}, u32[]{:S(2)}, u32[]{:S(2)}) collective-permute-start(bf16[6,2,128,128]{3,2,1,0:T(8,128)(2,1)S(1)} %add_convert_fusion.glob_one), channel_id=1, source_target_pairs={{32,64},{64,32},{96,0},{0,96},{33,65},{65,33},{97,1},{1,97},{34,66... | collective-permute-start | bytes 1179656 | tf_op jit(solution)/shard_map/ppermute | solution.py:379
  152.5 33.7 %all-to-all-start.3 = ((bf16[32,2,128,128]{3,2,1,0:T(8,128)(2,1)}), bf16[32,2,128,128]{3,2,1,0:T(8,128)(2,1)S(1)}, u32[]{:S(2)}, u32[]{:S(2)}) async-start(bf16[32,2,128,128]{3,2,1,0:T(8,128)(2,1)} %finish.1), calls=%async_computation.3 | async-start | bytes 4194304 | tf_op jit(solution)/shard_map/all_to_all | solution.py:337

commit v2 on v0

--- a/solution.py
+++ b/solution.py
@@ -16,7 +16,8 @@
 GLOB = 6
 BAND = WIN + 1
 UNIT = 3
-PART = 3
+STEPS = (3, 5, 6)
+ONES = 16
 NEG = -1e30
 SCALE = HD ** -0.5
 LOG2E = 1.4426950408889634
@@ -56,10 +57,10 @@
     for e in range(EXT):
         for ch in range(2):
             kt[ch, :, e * BLK:(e + 1) * BLK] = kx[ch, e].T
-            vt[ch, :, e * BLK:(e + 1) * BLK] = vx[ch, e].T
+            vt[ch, :HD, e * BLK:(e + 1) * BLK] = vx[ch, e].T
     for s in range(GLOB):
         kgt[:, s * BLK:(s + 1) * BLK] = glob[s, 0].T
-        vgt[:, s * BLK:(s + 1) * BLK] = glob[s, 1].T
+        vgt[:HD, s * BLK:(s + 1) * BLK] = glob[s, 1].T
 
     upper = lax.broadcasted_iota(jnp.int32, (1, 2 * BLK), 1) // BLK
     lane_full = lax.broadcasted_iota(jnp.int32, (BLK, 2 * BLK), 1)
@@ -119,18 +120,16 @@
                 r = first_r + k
                 off = jnp.where(allowed(r), keep["top"], -NEG)
                 e = jnp.exp2(st[slot, r * BLK:(r + 1) * BLK] * c - off)
-                here = jnp.sum(e.reshape(BLK // 8, 8, 2 * BLK), axis=0)
-                keep["total"] = keep["total"] + here if r else here
                 probs(first_r, n)[k * BLK:(k + 1) * BLK] = e.astype(BF16)
 
         cols = pl.ds(pl.multiple_of(t0 * BLK, 2 * BLK), cut)
 
         def attend():
-            keep["inv"] = inv = 1.0 / jnp.sum(keep["total"], axis=0, keepdims=True)
             ot = dot(vt[ch, :, cols], pb[tt])
             if wide:
                 ot = ot + dot(vgt[:, :wide], pg[slot, :wide])
-            ot = ot * inv
+            keep["inv"] = inv = 1.0 / ot[HD:HD + 1]
+            ot = ot[:HD] * inv
             ob = ot.astype(BF16)
             dof = dot_.astype(F32)
             keep["delta"] = jnp.sum(ob.astype(F32) * dof, axis=0, keepdims=True)
@@ -141,7 +140,7 @@
 
         def back(r, n):
             g = dot(source(vx, 1, r, n), dot_) - keep["delta"]
-            grads(r, n)[...] = (probs(r, n)[...].astype(F32) * g).astype(BF16)
+            grads(r, n)[...] = probs(r, n)[...] * g.astype(BF16)
 
         def finish_tile():
             dqt = dot(kt[ch, :, cols], ds[tt])
@@ -152,12 +151,14 @@
 
         return scores, after_scores, weigh, attend, back, finish_tile
 
+    vt[:, HD:] = jnp.ones((2, ONES, EXT * BLK + BLK), BF16)
+    vgt[HD:] = jnp.ones((ONES, GLOB * BLK), BF16)
     dkg[...] = jnp.zeros_like(dkg)
     dvg[...] = jnp.zeros_like(dvg)
 
     def group(ch, i, parts):
-        wide = parts * PART * BLK
-        segs = [(r, UNIT) for r in range(0, BAND, UNIT)] + [(BAND + PART * k, PART) for k in range(parts)]
+        wide = parts * BLK
+        segs = [(r, UNIT) for r in range(0, BAND, UNIT)] + [(BAND + k, min(UNIT, parts - k)) for k in range(0, parts, UNIT)]
         stages = [tile(ch, 4 * i + k, k, wide) for k in range(4)]
         scores, after_scores, weigh, attend, back, finish_tile = zip(*stages)
         for seg in segs:
@@ -188,9 +189,8 @@
             count = (info[4] <= last - w).astype(jnp.int32)
             for g in range(1, GLOB):
                 count += (info[4 + g] <= last - w).astype(jnp.int32)
-            needed = (count + PART - 1) // PART
-            for parts in range(GLOB // PART + 1):
-                @pl.when(needed == parts)
+            for least, parts in zip((-1,) + STEPS, STEPS):
+                @pl.when(jnp.logical_and(count > least, count <= parts))
                 def _(parts=parts):
                     group(ch, i, parts)
             return carry
@@ -264,9 +264,9 @@
             pltpu.VMEM((2, EXT, BLK, HD), BF16),
             pltpu.VMEM((2, EXT, BLK, HD), BF16),
             pltpu.VMEM((2, HD, EXT * BLK + BLK), BF16),
-            pltpu.VMEM((2, HD, EXT * BLK + BLK), BF16),
+            pltpu.VMEM((2, HD + ONES, EXT * BLK + BLK), BF16),
             pltpu.VMEM((HD, GLOB * BLK), BF16),
-            pltpu.VMEM((HD, GLOB * BLK), BF16),
+            pltpu.VMEM((HD + ONES, GLOB * BLK), BF16),
             pltpu.VMEM((RUN // 2, 2 * BLK, HD), BF16),
             pltpu.VMEM((RUN // 2, 2 * BLK, HD), BF16),
             pltpu.VMEM((4, (BAND + GLOB) * BLK, 2 * BLK), F32),

time: 188 us -> 186 us (0.989)
  no operation moved by 1% of the time
where the time goes in v2:
time: 186 us; the launch traced here: 184 us
  waiting for transfers between devices  61.4 us (33%)
  starting transfers between devices  51.2 us (28%)
  Pallas kernels  32.3 us (17%)
  local copies, waits for them, and re-layouts  19.4 us (10%)
  between operations  13.6 us (7%)
  other arithmetic  5.97 us (3%)
    all_to_all x4, waiting for transfers between devices, exchange(): return lax.all_to_all(x, GROUP, 0, 0, tiled=True)  37.9 us
    all_to_all x4, starting transfers between devices, exchange(): return lax.all_to_all(x, GROUP, 0, 0, tiled=True)  30.5 us
    pallas_call x1, Pallas kernels, attention(): pl.pallas_call(attention_kernel, out_shape=(sds((32, 2, BLK, HD), BF16),...  30 us
    slice x6, local copies, waits for them, and re-layouts, to_rows(): return (pair[0], pair[1])  10 us
    ppermute x1, waiting for transfers between devices, shards(): other = lax.ppermute(mine, 'y', PAIR_ONE)  9.04 us
    ppermute x1, waiting for transfers between devices, shards(): back_a = lax.ppermute(back_a, 'y', [(1, 0), (2, 1), (3, 2)])  8.5 us
    another operation x4, local copies, waits for them, and re-layouts, to_heads(): pair = jnp.stack([x, y], axis=0).reshape(2, BLK, 16, 2, HD)  6.37 us
    ppermute x1, starting transfers between devices, shards(): other = lax.ppermute(glob_grad, 'y', PAIR_ONE)  4.64 us
  transfers between devices with their start and end apart: 12, of which 9 were waited for; matrix products, arithmetic and copies ran while one was open for 9% of the time, Pallas kernels for 1%

profile of v2, /device:TPU:1, one launch (start us, length us, event | category | flops | bytes accessed | tf_op | source)
XLA Modules:
  0.0 184.0 jit_solution(207515435305456882)
XLA Ops:
  0.6 1.7 copy.18
  2.4 0.4 copy.19
  2.8 1.5 pad_maximum_fusion
  4.3 9.6 %all-to-all-start = ((bf16[32,2,128,128]{3,2,1,0:T(8,128)(2,1)}), bf16[32,2,128,128]{3,2,1,0:T(8,128)(2,1)S(1)}, u32[]{:S(2)}, u32[]{:S(2)}) async-start(bf16[32,2,128,128]{3,2,1,0:T(8,128)(2,1)} %bitcast.9), calls=%async_computation | async-start | bytes 4194304 | tf_op jit(solution)/shard_map/all_to_all | solution.py:337
  13.9 0.2 convert_reduce_fusion
  14.1 0.1 select_reduce_fusion
  14.2 0.6 fusion.5
  22.5 1.6 copy.20
  24.1 2.6 %copy.21 = bf16[1,128,16,2,128]{4,1,0,2,3:T(8,128)(2,1)} copy(bf16[1,128,16,2,128]{4,3,2,1,0:T(2,128)(2,1)} %bitcast.36) | data formatting | bytes 2097152 | tf_op jit(solution)/shard_map/stack | solution.py:325
  30.6 2.8 %pad_maximum_fusion.1 = bf16[2,128,16,2,128]{4,1,0,2,3:T(8,128)(2,1)} fusion(bf16[1,128,16,2,128]{4,1,0,2,3:T(8,128)(2,1)} %copy.21, bf16[1,128,16,2,128]{4,1,0,2,3:T(8,128)(2,1)S(1)} %copy.20), kind=kLoop, calls=%fused_computation.1 | loop fusion | flops 1048576 | bytes 4194304 | tf_op jit(solution)/shard_map/stack | solution.py:325
  33.4 8.8 %all-to-all-done.kv = bf16[32,2,128,128]{3,2,1,0:T(8,128)(2,1)S(1)} async-done(((bf16[32,2,128,128]{3,2,1,0:T(8,128)(2,1)}), bf16[32,2,128,128]{3,2,1,0:T(8,128)(2,1)S(1)}, u32[]{:S(2)}, u32[]{:S(2)}) %all-to-all-start) | async-done | bytes 2097184 | tf_op jit(solution)/shard_map/all_to_all | solution.py:337
  42.2 5.2 %all-to-all-start.1 = ((bf16[32,2,128,128]{3,2,1,0:T(8,128)(2,1)}), bf16[32,2,128,128]{3,2,1,0:T(8,128)(2,1)}, u32[]{:S(2)}, u32[]{:S(2)}) async-start(bf16[32,2,128,128]{3,2,1,0:T(8,128)(2,1)} %bitcast.13), calls=%async_computation.1 | async-start | bytes 4194304 | tf_op jit(solution)/shard_map/all_to_all | solution.py:337
  47.4 0.0 copy-start.3
  47.6 1.4 collective-permute-start.2
  49.0 9.0 %collective-permute-done.2 = bf16[6,2,128,128]{3,2,1,0:T(8,128)(2,1)S(1)} collective-permute-done((bf16[6,2,128,128]{3,2,1,0:T(8,128)(2,1)S(1)}, bf16[6,2,128,128]{3,2,1,0:T(8,128)(2,1)S(1)}, u32[]{:S(2)}, u32[]{:S(2)}) %collective-permute-start.2) | collective-permute-done | bytes 393248 | tf_op jit(solution)/shard_map/ppermute | solution.py:366
  58.0 0.1 broadcast_select_fusion
  58.1 2.8 %collective-permute-start.3 = (bf16[6,2,128,128]{3,2,1,0:T(8,128)(2,1)S(1)}, bf16[6,2,128,128]{3,2,1,0:T(8,128)(2,1)}, u32[]{:S(2)}, u32[]{:S(2)}) collective-permute-start(bf16[6,2,128,128]{3,2,1,0:T(8,128)(2,1)S(1)} %broadcast_select_fusion), channel_id=1, source_target_pairs={{32,64},{64,32},{96,0},{0,96},{33,65},{65,33},{97,1},{1,97},{34,66... | collective-permute-start | bytes 1179656 | tf_op jit(solution)/shard_map/ppermute | solution.py:368
  60.9 0.1 fusion.4
  61.0 1.3 collective-permute-start.1
  62.3 4.0 %collective-permute-start = (bf16[7,2,128,128]{3,2,1,0:T(8,128)(2,1)S(1)}, bf16[7,2,128,128]{3,2,1,0:T(8,128)(2,1)S(1)}, u32[]{:S(2)}, u32[]{:S(2)}) collective-permute-start(bf16[7,2,128,128]{3,2,1,0:T(8,128)(2,1)S(1)} %get-tuple-element.23), channel_id=1, source_target_pairs={{0,32},{32,64},{64,96},{1,33},{33,65},{65,97},{2,34},{34,66},{66,9... | collective-permute-start | bytes 1376264 | tf_op jit(solution)/shard_map/ppermute | solution.py:363
  66.4 0.6 fusion.6
  68.3 0.1 concatenate.8.info
  68.3 0.8 collective-permute-done.3
  69.1 1.1 broadcast_select_fusion.1.glob
  70.2 5.6 %all-to-all-done.1.qd = bf16[32,2,128,128]{3,2,1,0:T(8,128)(2,1)} async-done(((bf16[32,2,128,128]{3,2,1,0:T(8,128)(2,1)}), bf16[32,2,128,128]{3,2,1,0:T(8,128)(2,1)}, u32[]{:S(2)}, u32[]{:S(2)}) %all-to-all-start.1) | async-done | bytes 2097184 | tf_op jit(solution)/shard_map/all_to_all | solution.py:337
  75.8 0.0 collective-permute-done.1.halo_b
  75.8 0.8 copy-done.4
  76.6 0.8 copy-done.5
  77.4 30.0 %attention.1 = (bf16[32,2,128,128]{3,2,1,0:T(8,128)(2,1)}, bf16[32,2,128,128]{3,2,1,0:T(8,128)(2,1)}, bf16[7,2,128,128]{3,2,1,0:T(8,128)(2,1)S(1)}, bf16[7,2,128...) custom-call(s32[22]{0:T(128)S(1)} %concatenate.8.info, bf16[32,2,128,128]{3,2,1,0:T(8,128)(2,1)} %copy-done.1, ...), custom_call_target="tpu_custom_call" | custom-call | flops 11274289152 | bytes 16777216 | tf_op jit(solution)/shard_map/attention/pallas_call | solution.py:252
  107.3 7.8 %all-to-all-start.2 = ((bf16[32,2,128,128]{3,2,1,0:T(8,128)(2,1)}), bf16[32,2,128,128]{3,2,1,0:T(8,128)(2,1)}, u32[]{:S(2)}, u32[]{:S(2)}) async-start(bf16[32,2,128,128]{3,2,1,0:T(8,128)(2,1)} %get-tuple-element.9), calls=%async_computation.2 | async-start | bytes 4194304 | tf_op jit(solution)/shard_map/all_to_all | solution.py:337
  115.2 4.6 %collective-permute-start.6 = (bf16[6,2,128,128]{3,2,1,0:T(8,128)(2,1)S(1)}, bf16[6,2,128,128]{3,2,1,0:T(8,128)(2,1)S(1)}, u32[]{:S(2)}, u32[]{:S(2)}) collective-permute-start(bf16[6,2,128,128]{3,2,1,0:T(8,128)(2,1)S(1)} %get-tuple-element.13), channel_id=1, source_target_pairs={{0,32},{32,0},{64,96},{96,64},{1,33},{33,1},{65,97},{97,65},{2,34}... | collective-permute-start | bytes 1179656 | tf_op jit(solution)/shard_map/ppermute | solution.py:376
  119.8 1.3 collective-permute-start.4
  121.1 4.0 %collective-permute-start.5 = (bf16[7,2,128,128]{3,2,1,0:T(8,128)(2,1)S(1)}, bf16[7,2,128,128]{3,2,1,0:T(8,128)(2,1)S(1)}, u32[]{:S(2)}, u32[]{:S(2)}) collective-permute-start(bf16[7,2,128,128]{3,2,1,0:T(8,128)(2,1)S(1)} %get-tuple-element.12), channel_id=1, source_target_pairs={{0,32},{32,64},{64,96},{1,33},{33,65},{65,97},{2,34},{34,66},{66,9... | collective-permute-start | bytes 1376264 | tf_op jit(solution)/shard_map/ppermute | solution.py:375
  125.1 4.0 %collective-permute-done.6 = bf16[6,2,128,128]{3,2,1,0:T(8,128)(2,1)S(1)} collective-permute-done((bf16[6,2,128,128]{3,2,1,0:T(8,128)(2,1)S(1)}, bf16[6,2,128,128]{3,2,1,0:T(8,128)(2,1)S(1)}, u32[]{:S(2)}, u32[]{:S(2)}) %collective-permute-start.6) | collective-permute-done | bytes 393248 | tf_op jit(solution)/shard_map/ppermute | solution.py:376
  129.2 0.1 add_convert_fusion.glob_one
  129.3 1.2 collective-permute-start.7
  130.5 8.5 %collective-permute-done.4.back_a = bf16[7,2,128,128]{3,2,1,0:T(8,128)(2,1)S(1)} collective-permute-done((bf16[7,2,128,128]{3,2,1,0:T(8,128)(2,1)S(1)}, bf16[7,2,128,128]{3,2,1,0:T(8,128)(2,1)S(1)}, u32[]{:S(2)}, u32[]{:S(2)}) %collective-permute-start.4) | collective-permute-done | bytes 458784 | tf_op jit(solution)/shard_map/ppermute | solution.py:374
  139.0 1.2 collective-permute-done.7.glob_two
  140.2 2.4 %finish.1 = bf16[32,2,128,128]{3,2,1,0:T(8,128)(2,1)} custom-call(s32[22]{0:T(128)S(1)} %concatenate.8.info, bf16[32,2,128,128]{3,2,1,0:T(8,128)(2,1)S(1)} %copy-done, bf16[7,2,128,128]{3,2,1,0:T(8,128)(2,1)S(1)} %collective-permute-done.4.back_a, bf16[7,2,128,128]{3,2,1,0:T(8,128)(2,1)S(1)} %collective-permute-done.5.back_b, ...), custom_call_target="tpu_custom_call" | custom-call | flops 2097152 | bytes 6291456 | tf_op jit(solution)/shard_map/finish/pallas_call | solution.py:313
  142.5 1.0 all-to-all-done.2
  143.5 7.9 %all-to-all-start.3 = ((bf16[32,2,128,128]{3,2,1,0:T(8,128)(2,1)}), bf16[32,2,128,128]{3,2,1,0:T(8,128)(2,1)S(1)}, u32[]{:S(2)}, u32[]{:S(2)}) async-start(bf16[32,2,128,128]{3,2,1,0:T(8,128)(2,1)} %finish.1), calls=%async_computation.3 | async-start | bytes 4194304 | tf_op jit(solution)/shard_map/all_to_all | solution.py:337
  151.5 1.7 fusion.3
  153.2 2.0 %copy.23 = bf16[1,128,16,2,128]{4,3,2,1,0:T(2,128)(2,1)} copy(bf16[1,128,16,2,128]{4,1,0,2,3:T(8,128)(2,1)S(1)} %get-tuple-element.20) | data formatting | bytes 2097152 | tf_op jit(solution)/shard_map/slice | solution.py:333
  155.2 2.0 %copy.22 = bf16[1,128,16,2,128]{4,3,2,1,0:T(2,128)(2,1)} copy(bf16[1,128,16,2,128]{4,1,0,2,3:T(8,128)(2,1)S(1)} %get-tuple-element.21) | data formatting | bytes 2097152 | tf_op jit(solution)/shard_map/slice | solution.py:333
  157.3 22.5 %all-to-all-done.3 = bf16[32,2,128,128]{3,2,1,0:T(8,128)(2,1)S(1)} async-done(((bf16[32,2,128,128]{3,2,1,0:T(8,128)(2,1)}), bf16[32,2,128,128]{3,2,1,0:T(8,128)(2,1)S(1)}, u32[]{:S(2)}, u32[]{:S(2)}) %all-to-all-start.3) | async-done | bytes 2097184 | tf_op jit(solution)/shard_map/all_to_all | solution.py:337
  179.8 0.1 fusion.2
  179.9 2.0 %copy.25 = bf16[1,128,16,2,128]{4,3,2,1,0:T(2,128)(2,1)} copy(bf16[1,128,16,2,128]{4,1,0,2,3:T(8,128)(2,1)S(1)} %get-tuple-element.18) | data formatting | bytes 2097152 | tf_op jit(solution)/shard_map/slice | solution.py:333
  182.0 2.0 %copy.24 = bf16[1,128,16,2,128]{4,3,2,1,0:T(2,128)(2,1)} copy(bf16[1,128,16,2,128]{4,1,0,2,3:T(8,128)(2,1)S(1)} %get-tuple-element.19) | data formatting | bytes 2097152 | tf_op jit(solution)/shard_map/slice | solution.py:333
  (22 shorter events, 0.2 us)
Async XLA Ops:
  0.6 1.7 copy-start.2
  4.3 9.6 %copy-start.6 = (s32[6]{0:T(128)S(1)}, s32[6]{0:T(128)}, u32[]{:S(2)}) copy-start(s32[6]{0:T(128)} %param.11) | copy-start | bytes 76
  4.3 37.9 %all-to-all-start = ((bf16[32,2,128,128]{3,2,1,0:T(8,128)(2,1)}), bf16[32,2,128,128]{3,2,1,0:T(8,128)(2,1)S(1)}, u32[]{:S(2)}, u32[]{:S(2)}) async-start(bf16[32,2,128,128]{3,2,1,0:T(8,128)(2,1)} %bitcast.9), calls=%async_computation | async-start | bytes 4194304 | tf_op jit(solution)/shard_map/all_to_all | solution.py:337
  42.2 18.8 %copy-start.1 = (bf16[32,2,128,128]{3,2,1,0:T(8,128)(2,1)}, bf16[32,2,128,128]{3,2,1,0:T(8,128)(2,1)S(1)}, u32[]{:S(2)}) copy-start(bf16[32,2,128,128]{3,2,1,0:T(8,128)(2,1)S(1)} %all-to-all-done.kv) | copy-start | bytes 6291460
  42.2 33.6 %all-to-all-start.1 = ((bf16[32,2,128,128]{3,2,1,0:T(8,128)(2,1)}), bf16[32,2,128,128]{3,2,1,0:T(8,128)(2,1)}, u32[]{:S(2)}, u32[]{:S(2)}) async-start(bf16[32,2,128,128]{3,2,1,0:T(8,128)(2,1)} %bitcast.13), calls=%async_computation.1 | async-start | bytes 4194304 | tf_op jit(solution)/shard_map/all_to_all | solution.py:337
  47.4 19.0 %copy-start.3 = (s32[2]{0:T(128)S(1)}, s32[2]{0:T(128)}, u32[]{:S(2)}) copy-start(s32[2]{0:T(128)} %param.10) | copy-start | bytes 28
  47.6 10.5 %collective-permute-start.2 = (bf16[6,2,128,128]{3,2,1,0:T(8,128)(2,1)S(1)}, bf16[6,2,128,128]{3,2,1,0:T(8,128)(2,1)S(1)}, u32[]{:S(2)}, u32[]{:S(2)}) collective-permute-start(bf16[6,2,128,128]{3,2,1,0:T(8,128)(2,1)S(1)} %dynamic-slice_dynamic-update-slice_fusion), channel_id=1, source_target_pairs={{0,32},{32,0},{64,96},{96,64},{1,33},{33,1},{65,97},{97,65},{2,34}... | collective-permute-start | bytes 1179656 | tf_op jit(solution)/shard_map/ppermute | solution.py:366
  58.1 11.0 %collective-permute-start.3 = (bf16[6,2,128,128]{3,2,1,0:T(8,128)(2,1)S(1)}, bf16[6,2,128,128]{3,2,1,0:T(8,128)(2,1)}, u32[]{:S(2)}, u32[]{:S(2)}) collective-permute-start(bf16[6,2,128,128]{3,2,1,0:T(8,128)(2,1)S(1)} %broadcast_select_fusion), channel_id=1, source_target_pairs={{32,64},{64,32},{96,0},{0,96},{33,65},{65,33},{97,1},{1,97},{34,66... | collective-permute-start | bytes 1179656 | tf_op jit(solution)/shard_map/ppermute | solution.py:368
  61.0 14.8 %collective-permute-start.1 = (bf16[7,2,128,128]{3,2,1,0:T(8,128)(2,1)S(1)}, bf16[7,2,128,128]{3,2,1,0:T(8,128)(2,1)S(1)}, u32[]{:S(2)}, u32[]{:S(2)}) collective-permute-start(bf16[7,2,128,128]{3,2,1,0:T(8,128)(2,1)S(1)} %get-tuple-element.22), channel_id=1, source_target_pairs={{96,64},{64,32},{32,0},{97,65},{65,33},{33,1},{98,66},{66,34},{34,... | collective-permute-start | bytes 1376264 | tf_op jit(solution)/shard_map/ppermute | solution.py:364
  62.3 13.5 %collective-permute-start = (bf16[7,2,128,128]{3,2,1,0:T(8,128)(2,1)S(1)}, bf16[7,2,128,128]{3,2,1,0:T(8,128)(2,1)S(1)}, u32[]{:S(2)}, u32[]{:S(2)}) collective-permute-start(bf16[7,2,128,128]{3,2,1,0:T(8,128)(2,1)S(1)} %get-tuple-element.23), channel_id=1, source_target_pairs={{0,32},{32,64},{64,96},{1,33},{33,65},{65,97},{2,34},{34,66},{66,9... | collective-permute-start | bytes 1376264 | tf_op jit(solution)/shard_map/ppermute | solution.py:363
  75.8 0.8 copy-start.4
  76.6 0.8 copy-start.5
  107.3 32.8 %copy-start = (bf16[32,2,128,128]{3,2,1,0:T(8,128)(2,1)S(1)}, bf16[32,2,128,128]{3,2,1,0:T(8,128)(2,1)}, u32[]{:S(2)}) copy-start(bf16[32,2,128,128]{3,2,1,0:T(8,128)(2,1)} %get-tuple-element.10.own) | copy-start | bytes 6291460
  107.3 36.2 %all-to-all-start.2 = ((bf16[32,2,128,128]{3,2,1,0:T(8,128)(2,1)}), bf16[32,2,128,128]{3,2,1,0:T(8,128)(2,1)}, u32[]{:S(2)}, u32[]{:S(2)}) async-start(bf16[32,2,128,128]{3,2,1,0:T(8,128)(2,1)} %get-tuple-element.9), calls=%async_computation.2 | async-start | bytes 4194304 | tf_op jit(solution)/shard_map/all_to_all | solution.py:337
  115.2 14.0 %collective-permute-start.6 = (bf16[6,2,128,128]{3,2,1,0:T(8,128)(2,1)S(1)}, bf16[6,2,128,128]{3,2,1,0:T(8,128)(2,1)S(1)}, u32[]{:S(2)}, u32[]{:S(2)}) collective-permute-start(bf16[6,2,128,128]{3,2,1,0:T(8,128)(2,1)S(1)} %get-tuple-element.13), channel_id=1, source_target_pairs={{0,32},{32,0},{64,96},{96,64},{1,33},{33,1},{65,97},{97,65},{2,34}... | collective-permute-start | bytes 1179656 | tf_op jit(solution)/shard_map/ppermute | solution.py:376
  119.8 19.2 %collective-permute-start.4 = (bf16[7,2,128,128]{3,2,1,0:T(8,128)(2,1)S(1)}, bf16[7,2,128,128]{3,2,1,0:T(8,128)(2,1)S(1)}, u32[]{:S(2)}, u32[]{:S(2)}) collective-permute-start(bf16[7,2,128,128]{3,2,1,0:T(8,128)(2,1)S(1)} %get-tuple-element.11), channel_id=1, source_target_pairs={{32,0},{64,32},{96,64},{33,1},{65,33},{97,65},{34,2},{66,34},{98,6... | collective-permute-start | bytes 1376264 | tf_op jit(solution)/shard_map/ppermute | solution.py:374
  121.1 17.9 %collective-permute-start.5 = (bf16[7,2,128,128]{3,2,1,0:T(8,128)(2,1)S(1)}, bf16[7,2,128,128]{3,2,1,0:T(8,128)(2,1)S(1)}, u32[]{:S(2)}, u32[]{:S(2)}) collective-permute-start(bf16[7,2,128,128]{3,2,1,0:T(8,128)(2,1)S(1)} %get-tuple-element.12), channel_id=1, source_target_pairs={{0,32},{32,64},{64,96},{1,33},{33,65},{65,97},{2,34},{34,66},{66,9... | collective-permute-start | bytes 1376264 | tf_op jit(solution)/shard_map/ppermute | solution.py:375
  129.3 10.9 %collective-permute-start.7 = (bf16[6,2,128,128]{3,2,1,0:T(8,128)(2,1)S(1)}, bf16[6,2,128,128]{3,2,1,0:T(8,128)(2,1)S(1)}, u32[]{:S(2)}, u32[]{:S(2)}) collective-permute-start(bf16[6,2,128,128]{3,2,1,0:T(8,128)(2,1)S(1)} %add_convert_fusion.glob_one), channel_id=1, source_target_pairs={{32,64},{64,32},{96,0},{0,96},{33,65},{65,33},{97,1},{1,97},{34,66... | collective-permute-start | bytes 1179656 | tf_op jit(solution)/shard_map/ppermute | solution.py:378
  143.5 36.2 %all-to-all-start.3 = ((bf16[32,2,128,128]{3,2,1,0:T(8,128)(2,1)}), bf16[32,2,128,128]{3,2,1,0:T(8,128)(2,1)S(1)}, u32[]{:S(2)}, u32[]{:S(2)}) async-start(bf16[32,2,128,128]{3,2,1,0:T(8,128)(2,1)} %finish.1), calls=%async_computation.3 | async-start | bytes 4194304 | tf_op jit(solution)/shard_map/all_to_all | solution.py:337
